TPU v7x, 32 devices: a whole 2x2x4 slice. The times are simulated.
32 devices in a mesh: dap: 8 (over z, x), head: 4 (over y, core).
Axes of the slice: x: 2, y: 2, z: 4, core: 2. Of those that a mesh axis runs over, the one named last changes fastest.
Arguments:
- pair: bfloat16 [128, 128, 128], P('dap'), may hold values from -600 to 600
- residue_mask: int32 [128], replicated, may hold values 0 or 1
- chain_breaks: int32 [128], replicated, may hold values 0 or 1
- w_query: bfloat16 [128, 128], P(None, 'head'), may hold values from -0.5 to 0.5
- w_key: bfloat16 [128, 128], P(None, 'head'), may hold values from -0.5 to 0.5
- w_value: bfloat16 [128, 128], P(None, 'head'), may hold values from -0.5 to 0.5
- w_gate: bfloat16 [128, 128], P(None, 'head'), may hold values from -0.5 to 0.5
- w_bias: bfloat16 [128, 4], P(None, 'head'), may hold values from -29 to 29
- w_out: bfloat16 [128, 128], P('head'), may hold values from -0.5 to 0.5
Outputs:
- update: bfloat16 [128, 128, 128], P('dap', None, 'head')
All inputs are finite; a program needn't handle non-finite values.
Results may differ from a plain program's by a relative error of at most 0.019.
Values may be sent and summed in bfloat16 or wider, within the bound.
A program may use at most 64 MiB of HBM per device.

v0:
```python
import functools

import jax
import jax.numpy as jnp
from jax import lax
from jax.experimental import pallas as pl
from jax.experimental.pallas import tpu as pltpu
from jax.sharding import PartitionSpec as P

chain_penalty = 2.0
masked_score = -1000000000.0
LANES = 128
MESH = pl.DeviceIdType.MESH
f32 = jnp.float32
bf16 = jnp.bfloat16


def nn(a, b):
    return lax.dot_general(a, b, (((1,), (0,)), ((), ())), preferred_element_type=f32)


def nt(a, b):
    return lax.dot_general(a, b, (((1,), (1,)), ((), ())), preferred_element_type=f32)


def tn(a, b):
    return lax.dot_general(a, b, (((0,), (0,)), ((), ())), preferred_element_type=f32)


def each(count, do, start=0, most=8):
    if count - start <= most:
        for index in range(start, count):
            do(index)
    else:
        pl.loop(start, count)(do)


def lanes_at(place):
    return pl.ds(pl.multiple_of(place * LANES, LANES), LANES)


def ones_where(condition):
    return jnp.where(condition, 1.0, 0.0).astype(bf16)


def iota(shape, axis):
    return lax.broadcasted_iota(jnp.int32, shape, axis)


def normalize(x, average):
    mean = nn(x, average)
    centered = x.astype(f32) - mean
    square = centered * centered
    high = square.astype(bf16)
    low = (square - high.astype(f32)).astype(bf16)
    variance = nn(high, average) + nn(low, average)
    return (centered * lax.rsqrt(variance + 1e-05)).astype(bf16)


def kernel(
    groups, heads,
    pair_in, mask_in, breaks_in, wq, wk, wv, wg, wb_in, wo,
    out,
    pair, mask, breaks, wb, stage, x, weights, wb_all, bias, wide, chain_column, chain_row, keep,
    query, keys, values_t, gate_t, gated, result, landed, leave, arrive,
    in_sem, x_sem, w_sem, wb_sem, b_sem, r_sem,
):
    rows, total, channels = pair.shape
    width = wq.shape[0]
    devices = groups * heads
    block = total // groups
    columns = total // devices
    d = lax.axis_index("dap")
    h = lax.axis_index("head")
    me = d * heads + h
    my_rows = pl.ds(pl.multiple_of(d * rows, rows), rows)

    def around(place, offset, count):
        moved = place + offset
        return jnp.where(moved >= count, moved - count, moved)

    def others(do):
        for offset in range(1, heads):
            do(d, around(h, offset, heads))

        def at_group(offset):
            group = around(d, offset, groups)
            for head_offset in range(heads):
                do(group, around(h, head_offset, heads))

        pl.loop(1, groups)(at_group)

    loads = [
        pltpu.make_async_copy(source, target, in_sem.at[place])
        for place, (source, target) in enumerate(
            [(pair_in, pair), (wb_in, wb)]
            + [
                (matrix, weights.at[h, place * width : (place + 1) * width, :])
                for place, matrix in enumerate((wq, wk, wv, wg, wo))
            ]
            + [(mask_in, mask), (breaks_in, breaks)]
        )
    ]
    for load in loads:
        load.start()

    barrier = pltpu.get_barrier_semaphore()

    def greet(pd, ph):
        pl.semaphore_signal(barrier, inc=1, device_id=(pd, ph), device_id_type=MESH)

    others(greet)

    taken = columns * rows
    in_row = iota((1, rows * block), 1)
    column = lax.rem(in_row, block) - h * columns
    wanted = jnp.where((column >= 0) & (column < columns), column * rows + in_row // block, -1)
    select = ones_where(iota((taken, rows * block), 0) == wanted)
    loads[0].wait()

    def selected(group):
        part = pair[:, pl.ds(pl.multiple_of(group * block, block), block), :]
        return nn(select, part.reshape(rows * block, channels)).astype(bf16)

    def fill(offset):
        part = selected(around(d, offset, groups))
        stage[offset] = part.reshape(columns, rows, channels)

    each(groups, fill, start=1)
    x[:, my_rows, :] = selected(d).reshape(columns, rows, channels)

    for load in loads[1:]:
        load.wait()
    wb_all[h] = jnp.broadcast_to(wb[...].astype(f32), (rows, channels)).astype(bf16)
    pl.semaphore_wait(barrier, devices - 1)

    def send(source, target, sems, pd, ph):
        return pltpu.make_async_remote_copy(
            src_ref=source,
            dst_ref=target,
            send_sem=sems.at[0],
            recv_sem=sems.at[1],
            device_id=(pd, ph),
            device_id_type=MESH,
        )

    def all_copies(part, sems):
        return send(part, part, sems, d, around(h, 1, heads))

    all_x = all_copies(stage.at[pl.ds(0, groups - 1)], x_sem)
    all_w = all_copies(weights.at[pl.ds(0, heads - 1)], w_sem)
    all_wb = all_copies(wb_all.at[pl.ds(0, heads - 1)], wb_sem)
    all_b = all_copies(bias.at[:, pl.ds(0, (groups - 1) * rows), :], b_sem)
    all_r = all_copies(landed.at[pl.ds(0, devices - 1)], r_sem)

    for offset in range(1, heads):
        send(wb_all.at[h], wb_all.at[h], wb_sem, d, around(h, offset, heads)).start()

    @pl.loop(1, groups)
    def _(offset):
        send(stage.at[offset], x.at[:, my_rows, :], x_sem, around(d, offset, groups), h).start()

    for offset in range(1, heads):
        send(weights.at[h], weights.at[h], w_sem, d, around(h, offset, heads)).start()

    average = jnp.full((channels, channels), 1.0 / channels, f32).astype(bf16)
    bias_row = lax.rem(iota((heads * rows, LANES), 0), rows)

    def bias_block(place, arrived=True):
        span = lanes_at(place)
        entries = pair[:, span, :].reshape(rows * LANES, channels)
        normed = normalize(entries, average)
        if not arrived:
            all_wb.wait_recv()
        wb_rows = wb_all[...].reshape(heads * rows, channels)
        found = jnp.zeros((heads * rows, LANES), f32)
        for row in range(rows):
            line = nt(wb_rows, normed[row * LANES : (row + 1) * LANES])
            found = jnp.where(bias_row == row, line, found)
        bias[:, my_rows, span] = found.astype(bf16).reshape(heads, rows, LANES)

    bias_block(0, arrived=False)
    if total > LANES:
        pl.loop(1, total // LANES)(bias_block)

    @pl.loop(1, groups)
    def _(offset):
        part = bias.at[:, my_rows, :]
        send(part, part, b_sem, around(d, offset, groups), h).start()

    tall = iota((total, total), 0)
    across = iota((total, total), 1)
    breaks_row = jnp.broadcast_to(breaks[...].astype(f32), (LANES, total)).astype(bf16)
    mask_row = jnp.broadcast_to(mask[...].astype(f32), (LANES, total)).astype(bf16)
    chain_column[...] = nt(ones_where(across <= tall), breaks_row)
    keep[...] = nt(ones_where(across == tall), mask_row)
    chain_row[...] = nn(breaks_row[:8], ones_where(tall <= across))

    out_lanes = heads * columns * width
    lane = iota((1, out_lanes), 1)
    lane_column = lax.rem(lane, columns * width) // width
    lane_source = lane // (columns * width) * width + lax.rem(lane, width)
    channel = iota((channels, out_lanes), 0)

    ordered = columns * LANES
    first = iota((ordered, ordered), 0)
    second = iota((1, ordered), 1)
    entry = lax.rem(second, LANES)
    leave[...] = ones_where(
        first
        == lax.rem(entry, columns) * LANES + entry // columns * columns + second // LANES
    )
    arrive[...] = ones_where(
        first
        == entry // columns * rows + second // LANES * columns + lax.rem(entry, columns)
    )

    all_w.wait_recv()
    wo_full = jnp.concatenate([weights[k, 4 * width : 5 * width, :] for k in range(heads)], axis=0)
    for column in range(columns):
        placed = ones_where(channel == jnp.where(lane_column == column, lane_source, -1))
        wide[column * channels : (column + 1) * channels, :] = nn(wo_full, placed).astype(bf16)
    wq_t, wk_t, wv_t, wg_t = (
        jnp.concatenate(
            [weights[k, place * width : (place + 1) * width, :] for k in range(heads)], axis=0
        )
        for place in range(4)
    )

    all_x.wait_recv()
    for column in range(columns):
        normed = normalize(x[column], average)
        query[column] = (nt(normed, wq_t) * width ** (-0.5)).astype(bf16)
        keys[column] = nt(normed, wk_t).astype(bf16)
        values_t[column] = nt(wv_t, normed).astype(bf16)
        gate_t[column] = jax.nn.sigmoid(nt(wg_t, normed)).astype(bf16)

    all_b.wait_recv()
    head_of_lane = iota((total, heads * width), 1) // width

    def attend(place):
        span = lanes_at(place)
        penalty = jnp.where(chain_column[...] == chain_row[:1, span], 0.0, -chain_penalty)
        for head in range(heads):
            added = bias[head, :, span].astype(f32) + penalty
            share_t = slice(head * width, (head + 1) * width)

            def attend_column(column):
                own = keys[column]
                own = jnp.where(head_of_lane == head, own, jnp.zeros_like(own))
                scores = nt(own, query[column, span, :]) + added
                scores = jnp.where(keep[...] > 0.5, scores, masked_score)
                expo = jnp.exp(scores - jnp.max(scores, axis=0, keepdims=True))
                scale = 1.0 / jnp.sum(expo, axis=0, keepdims=True)
                attended = nn(values_t[column, share_t, :], (expo * scale).astype(bf16))
                gated[column, share_t, span] = (
                    gate_t[column, share_t, span].astype(f32) * attended.astype(bf16).astype(f32)
                ).astype(bf16)

            each(columns, attend_column, most=columns if total == LANES else 1)

    each(total // LANES, attend, most=1)

    packed_lanes = columns * width

    def project(place):
        span = lanes_at(place)
        mine = jnp.concatenate([gated[column, :, span] for column in range(columns)], axis=1)
        mine = nt(leave[...], mine).astype(bf16)
        mine = jnp.concatenate(
            [mine[part * LANES : (part + 1) * LANES] for part in range(columns)], axis=1
        )
        update = nn(mine, wide[...]).astype(bf16)
        for part in range(LANES // rows):
            for head in range(heads):
                result[(place * (LANES // rows) + part) * heads + head] = update[
                    part * rows : (part + 1) * rows,
                    head * packed_lanes : (head + 1) * packed_lanes,
                ]

    each(total // LANES, project, most=1)

    def give(pd, ph):
        send(result.at[pd * heads + ph], landed.at[me], r_sem, pd, ph).start()

    others(give)
    landed[me] = result[me]
    for copies in (all_x, all_w, all_wb, all_b):
        copies.wait_send()
    all_r.wait_recv()
    sources = LANES // columns

    def settle(place):
        came = landed[pl.ds(place * sources, sources)].reshape(sources * rows, packed_lanes)
        moved = tn(came, arrive[...]).astype(bf16)
        for row in range(rows):
            part, line = row // columns, row % columns
            out[row, :, lanes_at(place)] = moved[
                line * width : (line + 1) * width, part * LANES : (part + 1) * LANES
            ]

    each(total // LANES, settle, most=1)
    all_r.wait_send()


def body(groups, heads, pair, residue_mask, chain_breaks, w_query, w_key, w_value, w_gate, w_bias, w_out):
    rows, total, channels = pair.shape
    width = w_query.shape[1]
    devices = groups * heads
    columns = total // devices
    packed_lanes = columns * width
    assert packed_lanes == LANES and columns * columns == rows
    dma = pltpu.SemaphoreType.DMA
    update = pl.pallas_call(
        functools.partial(kernel, groups, heads),
        out_shape=jax.ShapeDtypeStruct((rows, width, total), bf16),
        in_specs=[pl.BlockSpec(memory_space=pltpu.HBM)] * 9,
        out_specs=pl.BlockSpec(memory_space=pltpu.VMEM),
        scratch_shapes=[
            pltpu.VMEM((rows, total, channels), bf16),
            pltpu.VMEM((1, total), jnp.int32),
            pltpu.VMEM((1, total), jnp.int32),
            pltpu.VMEM((1, channels), bf16),
            pltpu.VMEM((groups, columns, rows, channels), bf16),
            pltpu.VMEM((columns, total, channels), bf16),
            pltpu.VMEM((heads, 5 * width, channels), bf16),
            pltpu.VMEM((heads, rows, channels), bf16),
            pltpu.VMEM((heads, total, total), bf16),
            pltpu.VMEM((columns * channels, heads * packed_lanes), bf16),
            pltpu.VMEM((total, LANES), f32),
            pltpu.VMEM((8, total), f32),
            pltpu.VMEM((total, LANES), f32),
            pltpu.VMEM((columns, total, channels), bf16),
            pltpu.VMEM((columns, total, channels), bf16),
            pltpu.VMEM((columns, channels, total), bf16),
            pltpu.VMEM((columns, channels, total), bf16),
            pltpu.VMEM((columns, channels, total), bf16),
            pltpu.VMEM((devices, rows, packed_lanes), bf16),
            pltpu.VMEM((devices, rows, packed_lanes), bf16),
            pltpu.VMEM((columns * LANES, columns * LANES), bf16),
            pltpu.VMEM((columns * LANES, columns * LANES), bf16),
            dma((9,)), dma((2,)), dma((2,)), dma((2,)), dma((2,)), dma((2,)),
        ],
        compiler_params=pltpu.CompilerParams(
            collective_id=0, has_side_effects=True, vmem_limit_bytes=58 * 2**20
        ),
    )(
        pair, residue_mask.reshape(1, total), chain_breaks.reshape(1, total),
        w_query.T, w_key.T, w_value.T, w_gate.T, w_bias.T, w_out,
    )
    return jnp.swapaxes(update, 1, 2)


def solution(mesh):
    placed = (
        P("dap", None, None),
        P(),
        P(),
        P(None, "head"),
        P(None, "head"),
        P(None, "head"),
        P(None, "head"),
        P(None, "head"),
        P("head", None),
    )
    return jax.shard_map(
        functools.partial(body, mesh.shape["dap"], mesh.shape["head"]),
        mesh=mesh, in_specs=placed, out_specs=P("dap", None, "head"), check_vma=False,
    )
```

profile of v0, /device:TPU:0, one launch (start us, length us, event | category | flops | bytes accessed | tf_op | source)
XLA Modules:
  0.0 27.0 jit_solution(10447885790629872010)
XLA Ops:
  0.0 25.4 %shard_map.91 = bf16[16,32,128]{2,1,0:T(8,128)(2,1)} custom-call(bf16[16,128,128]{2,1,0:T(8,128)(2,1)} %pair_in.1, s32[1,128]{1,0:T(1,128)} %bitcast.13, s32[1,128]{1,0:T(1,128)} %bitcast.14, bf16[32,128]{1,0:T(8,128)(2,1)} %bitcast.9, bf16[32,128]{1,0:T(8,128)(2,1)} %bitcast.10, bf16[32,128]{1,0:T(8,128)(2,1)} %bitcast.11, bf16[32,128]{1,0:T(8,128)(2,1)} %bitcast.12, ...), custom_call_target="tpu_custom_call" | custom-call | tf_op jit(solution)/shard_map/pallas_call | solution.py:314
  25.4 1.6 %copy.11 = bf16[16,128,32]{1,2,0:T(8,128)(2,1)} copy(bf16[16,128,32]{1,2,0:T(8,128)(2,1)} %bitcast.8) | data formatting | bytes 262144
where the time goes:
time: 27.1 us; the launch traced here: 27 us
  Pallas kernels  25.4 us (94%)
  local copies, waits for them, and re-layouts  1.57 us (6%)
    pallas_call x1, Pallas kernels, body(): pl.pallas_call(functools.partial(kernel, groups, heads), out_shape=jax.Sh...  25.4 us
    unnamed x1, local copies, waits for them, and re-layouts  1.57 us

commit v1 on v0

--- a/solution.py
+++ b/solution.py
@@ -79,16 +79,8 @@
         moved = place + offset
         return jnp.where(moved >= count, moved - count, moved)
 
-    def others(do):
-        for offset in range(1, heads):
-            do(d, around(h, offset, heads))
-
-        def at_group(offset):
-            group = around(d, offset, groups)
-            for head_offset in range(heads):
-                do(group, around(h, head_offset, heads))
-
-        pl.loop(1, groups)(at_group)
+    def far(step):
+        return around(d, lax.rem(step + groups // 2 - 2, groups - 1) + 1, groups)
 
     loads = [
         pltpu.make_async_copy(source, target, in_sem.at[place])
@@ -101,38 +93,32 @@
             + [(mask_in, mask), (breaks_in, breaks)]
         )
     ]
-    for load in loads:
-        load.start()
+    loads[0].start()
 
     barrier = pltpu.get_barrier_semaphore()
 
     def greet(pd, ph):
         pl.semaphore_signal(barrier, inc=1, device_id=(pd, ph), device_id_type=MESH)
 
-    others(greet)
+    each(groups, lambda step: greet(far(step), h), start=1)
+    each(heads, lambda offset: greet(d, around(h, offset, heads)), start=1)
+    for load in loads[1:]:
+        load.start()
 
     taken = columns * rows
     in_row = iota((1, rows * block), 1)
     column = lax.rem(in_row, block) - h * columns
     wanted = jnp.where((column >= 0) & (column < columns), column * rows + in_row // block, -1)
     select = ones_where(iota((taken, rows * block), 0) == wanted)
-    loads[0].wait()
 
     def selected(group):
         part = pair[:, pl.ds(pl.multiple_of(group * block, block), block), :]
-        return nn(select, part.reshape(rows * block, channels)).astype(bf16)
-
-    def fill(offset):
-        part = selected(around(d, offset, groups))
-        stage[offset] = part.reshape(columns, rows, channels)
-
-    each(groups, fill, start=1)
-    x[:, my_rows, :] = selected(d).reshape(columns, rows, channels)
-
-    for load in loads[1:]:
-        load.wait()
+        part = nn(select, part.reshape(rows * block, channels)).astype(bf16)
+        return part.reshape(columns, rows, channels)
+
+    loads[1].wait()
     wb_all[h] = jnp.broadcast_to(wb[...].astype(f32), (rows, channels)).astype(bf16)
-    pl.semaphore_wait(barrier, devices - 1)
+    pl.semaphore_wait(barrier, groups + heads - 2)
 
     def send(source, target, sems, pd, ph):
         return pltpu.make_async_remote_copy(
@@ -156,10 +142,17 @@
     for offset in range(1, heads):
         send(wb_all.at[h], wb_all.at[h], wb_sem, d, around(h, offset, heads)).start()
 
-    @pl.loop(1, groups)
-    def _(offset):
-        send(stage.at[offset], x.at[:, my_rows, :], x_sem, around(d, offset, groups), h).start()
-
+    loads[0].wait()
+
+    def scatter(step):
+        group = far(step)
+        stage[step] = selected(group)
+        send(stage.at[step], x.at[:, my_rows, :], x_sem, group, h).start()
+
+    each(groups, scatter, start=1)
+    x[:, my_rows, :] = selected(d)
+    for load in loads[2:]:
+        load.wait()
     for offset in range(1, heads):
         send(weights.at[h], weights.at[h], w_sem, d, around(h, offset, heads)).start()
 
@@ -168,25 +161,24 @@
 
     def bias_block(place, arrived=True):
         span = lanes_at(place)
-        entries = pair[:, span, :].reshape(rows * LANES, channels)
-        normed = normalize(entries, average)
+        normed = [normalize(pair[row, span, :], average) for row in range(rows)]
         if not arrived:
             all_wb.wait_recv()
         wb_rows = wb_all[...].reshape(heads * rows, channels)
         found = jnp.zeros((heads * rows, LANES), f32)
         for row in range(rows):
-            line = nt(wb_rows, normed[row * LANES : (row + 1) * LANES])
-            found = jnp.where(bias_row == row, line, found)
+            found = jnp.where(bias_row == row, nt(wb_rows, normed[row]), found)
         bias[:, my_rows, span] = found.astype(bf16).reshape(heads, rows, LANES)
 
     bias_block(0, arrived=False)
     if total > LANES:
         pl.loop(1, total // LANES)(bias_block)
 
-    @pl.loop(1, groups)
-    def _(offset):
+    def share_bias(step):
         part = bias.at[:, my_rows, :]
-        send(part, part, b_sem, around(d, offset, groups), h).start()
+        send(part, part, b_sem, far(step), h).start()
+
+    each(groups, share_bias, start=1)
 
     tall = iota((total, total), 0)
     across = iota((total, total), 1)
@@ -283,7 +275,10 @@
     def give(pd, ph):
         send(result.at[pd * heads + ph], landed.at[me], r_sem, pd, ph).start()
 
-    others(give)
+    for head_offset in range(heads):
+        head = around(h, head_offset, heads)
+        each(groups, lambda step, head=head: give(far(step), head), start=1)
+    each(heads, lambda offset: give(d, around(h, offset, heads)), start=1)
     landed[me] = result[me]
     for copies in (all_x, all_w, all_wb, all_b):
         copies.wait_send()
@@ -313,7 +308,7 @@
     dma = pltpu.SemaphoreType.DMA
     update = pl.pallas_call(
         functools.partial(kernel, groups, heads),
-        out_shape=jax.ShapeDtypeStruct((rows, width, total), bf16),
+        out_shape=pltpu.VMEM((rows, width, total), bf16),
         in_specs=[pl.BlockSpec(memory_space=pltpu.HBM)] * 9,
         out_specs=pl.BlockSpec(memory_space=pltpu.VMEM),
         scratch_shapes=[
@@ -342,11 +337,16 @@
             dma((9,)), dma((2,)), dma((2,)), dma((2,)), dma((2,)), dma((2,)),
         ],
         compiler_params=pltpu.CompilerParams(
-            collective_id=0, has_side_effects=True, vmem_limit_bytes=58 * 2**20
+            collective_id=0, has_side_effects=True, vmem_limit_bytes=52 * 2**20
         ),
     )(
-        pair, residue_mask.reshape(1, total), chain_breaks.reshape(1, total),
-        w_query.T, w_key.T, w_value.T, w_gate.T, w_bias.T, w_out,
+        *(
+            pltpu.with_memory_space_constraint(operand, pltpu.HBM)
+            for operand in (
+                pair, residue_mask.reshape(1, total), chain_breaks.reshape(1, total),
+                w_query.T, w_key.T, w_value.T, w_gate.T, w_bias.T, w_out,
+            )
+        )
     )
     return jnp.swapaxes(update, 1, 2)
 

time: 27.1 us -> 24.7 us (0.911)
  Pallas kernels: 25.4 us -> 23.9 us
  local copies, waits for them, and re-layouts: 1.57 us -> 0.66 us
    pallas_call x1, Pallas kernels: 25.4 us -> 23.9 us  [body(): pl.pallas_call(functools.partial(kernel, groups, heads), out_shape=pltpu....]
    unnamed x1, local copies, waits for them, and re-layouts: 1.57 us -> 0.66 us
where the time goes in v1:
time: 24.7 us; the launch traced here: 24.6 us
  Pallas kernels  23.9 us (97%)
  local copies, waits for them, and re-layouts  0.66 us (3%)
    pallas_call x1, Pallas kernels, body(): pl.pallas_call(functools.partial(kernel, groups, heads), out_shape=pltpu....  23.9 us
    unnamed x1, local copies, waits for them, and re-layouts  0.66 us

profile of v1, /device:TPU:0, one launch (start us, length us, event | category | flops | bytes accessed | tf_op | source)
XLA Modules:
  0.0 24.6 jit_solution(13065957283082681910)
XLA Ops:
  0.0 23.9 %shard_map.91 = bf16[16,32,128]{2,1,0:T(8,128)(2,1)S(1)} custom-call(bf16[16,128,128]{2,1,0:T(8,128)(2,1)} %pair_in.1, s32[1,128]{1,0:T(1,128)} %bitcast.13, s32[1,128]{1,0:T(1,128)} %bitcast.14, bf16[32,128]{1,0:T(8,128)(2,1)} %bitcast.9, bf16[32,128]{1,0:T(8,128)(2,1)} %bitcast.10, bf16[32,128]{1,0:T(8,128)(2,1)} %bitcast.11, bf16[32,128]{1,0:T(8,128)(2,1)} %bitcast.12, ...), custom_call_target="tpu_custom_call" | custom-call | tf_op jit(solution)/shard_map/pallas_call | solution.py:309
  23.9 0.7 %copy.11 = bf16[16,128,32]{1,2,0:T(8,128)(2,1)} copy(bf16[16,128,32]{1,2,0:T(8,128)(2,1)S(1)} %bitcast.8) | data formatting | bytes 262144

commit v2 on v1

--- a/solution.py
+++ b/solution.py
@@ -218,38 +218,55 @@
         )
         for place in range(4)
     )
+    wqk_t = jnp.concatenate([wq_t, wk_t], axis=0)
+    wvg_t = jnp.concatenate([wv_t, wg_t], axis=0)
+    wide_heads = heads * width
 
     all_x.wait_recv()
-    for column in range(columns):
-        normed = normalize(x[column], average)
-        query[column] = (nt(normed, wq_t) * width ** (-0.5)).astype(bf16)
-        keys[column] = nt(normed, wk_t).astype(bf16)
-        values_t[column] = nt(wv_t, normed).astype(bf16)
-        gate_t[column] = jax.nn.sigmoid(nt(wg_t, normed)).astype(bf16)
+    def project_in(first, count):
+        normed = normalize(x[first : first + count].reshape(count * total, channels), average)
+        upright = nt(normed, wqk_t)
+        turned = nt(wvg_t, normed)
+        for column in range(count):
+            part = slice(column * total, (column + 1) * total)
+            query[first + column] = (upright[part, :wide_heads] * width ** (-0.5)).astype(bf16)
+            keys[first + column] = upright[part, wide_heads:].astype(bf16)
+            values_t[first + column] = turned[:wide_heads, part].astype(bf16)
+            gate_t[first + column] = jax.nn.sigmoid(turned[wide_heads:, part]).astype(bf16)
+
+    together = columns if total == LANES else 1
+    for first in range(0, columns, together):
+        project_in(first, together)
 
     all_b.wait_recv()
-    head_of_lane = iota((total, heads * width), 1) // width
+    head_of_lane = iota((total, wide_heads), 1) // width
+    head_of_row = iota((wide_heads, total), 0) // width
 
     def attend(place):
         span = lanes_at(place)
         penalty = jnp.where(chain_column[...] == chain_row[:1, span], 0.0, -chain_penalty)
-        for head in range(heads):
-            added = bias[head, :, span].astype(f32) + penalty
-            share_t = slice(head * width, (head + 1) * width)
-
-            def attend_column(column):
-                own = keys[column]
-                own = jnp.where(head_of_lane == head, own, jnp.zeros_like(own))
-                scores = nt(own, query[column, span, :]) + added
-                scores = jnp.where(keep[...] > 0.5, scores, masked_score)
-                expo = jnp.exp(scores - jnp.max(scores, axis=0, keepdims=True))
+        added = [bias[head, :, span].astype(f32) + penalty for head in range(heads)]
+        present = keep[...] > 0.5
+
+        def attend_column(column):
+            upright, turned = keys[column], values_t[column]
+            nothing = jnp.zeros((), bf16)
+            own = [jnp.where(head_of_lane == head, upright, nothing) for head in range(heads)]
+            scores = nt(jnp.concatenate(own, axis=0), query[column, span, :])
+            shares = []
+            for head in range(heads):
+                mine = scores[head * total : (head + 1) * total] + added[head]
+                mine = jnp.where(present, mine, masked_score)
+                expo = jnp.exp(mine - jnp.max(mine, axis=0, keepdims=True))
                 scale = 1.0 / jnp.sum(expo, axis=0, keepdims=True)
-                attended = nn(values_t[column, share_t, :], (expo * scale).astype(bf16))
-                gated[column, share_t, span] = (
-                    gate_t[column, share_t, span].astype(f32) * attended.astype(bf16).astype(f32)
-                ).astype(bf16)
-
-            each(columns, attend_column, most=columns if total == LANES else 1)
+                shares.append((expo * scale).astype(bf16))
+            own = [jnp.where(head_of_row == head, turned, nothing) for head in range(heads)]
+            attended = nn(jnp.concatenate(own, axis=1), jnp.concatenate(shares, axis=0))
+            gated[column, :, span] = (
+                gate_t[column, :, span].astype(f32) * attended.astype(bf16).astype(f32)
+            ).astype(bf16)
+
+        each(columns, attend_column, most=columns if total == LANES else 1)
 
     each(total // LANES, attend, most=1)
 

time: 24.7 us -> 22 us (0.89)
  Pallas kernels: 23.9 us -> 21.2 us
    pallas_call x1, Pallas kernels: 23.9 us -> 21.2 us  [body(): pl.pallas_call(functools.partial(kernel, groups, heads), out_shape=pltpu....]
where the time goes in v2:
time: 22 us; the launch traced here: 21.9 us
  Pallas kernels  21.2 us (96%)
  local copies, waits for them, and re-layouts  0.66 us (3%)
    pallas_call x1, Pallas kernels, body(): pl.pallas_call(functools.partial(kernel, groups, heads), out_shape=pltpu....  21.2 us
    unnamed x1, local copies, waits for them, and re-layouts  0.66 us

profile of v2, /device:TPU:0, one launch (start us, length us, event | category | flops | bytes accessed | tf_op | source)
XLA Modules:
  0.0 21.9 jit_solution(5465795063228871157)
XLA Ops:
  0.0 21.2 %shard_map.91 = bf16[16,32,128]{2,1,0:T(8,128)(2,1)S(1)} custom-call(bf16[16,128,128]{2,1,0:T(8,128)(2,1)} %pair_in.1, s32[1,128]{1,0:T(1,128)} %bitcast.13, s32[1,128]{1,0:T(1,128)} %bitcast.14, bf16[32,128]{1,0:T(8,128)(2,1)} %bitcast.9, bf16[32,128]{1,0:T(8,128)(2,1)} %bitcast.10, bf16[32,128]{1,0:T(8,128)(2,1)} %bitcast.11, bf16[32,128]{1,0:T(8,128)(2,1)} %bitcast.12, ...), custom_call_target="tpu_custom_call" | custom-call | tf_op jit(solution)/shard_map/pallas_call | solution.py:326
  21.2 0.7 %copy.11 = bf16[16,128,32]{1,2,0:T(8,128)(2,1)} copy(bf16[16,128,32]{1,2,0:T(8,128)(2,1)S(1)} %bitcast.8) | data formatting | bytes 262144

commit v3 on v2

--- a/solution.py
+++ b/solution.py
@@ -63,7 +63,7 @@
     out,
     pair, mask, breaks, wb, stage, x, weights, wb_all, bias, wide, chain_column, chain_row, keep,
     query, keys, values_t, gate_t, gated, result, landed, leave, arrive,
-    in_sem, x_sem, w_sem, wb_sem, b_sem, r_sem,
+    pair_sem, in_sem, x_sem, w_sem, wb_sem, b_sem, p_sem, r_sem,
 ):
     rows, total, channels = pair.shape
     width = wq.shape[0]
@@ -73,6 +73,10 @@
     d = lax.axis_index("dap")
     h = lax.axis_index("head")
     me = d * heads + h
+    half_heads = heads // 2
+    mine_first = lax.rem(h, 2) * half_heads
+    partner = h + 1 - 2 * lax.rem(h, 2)
+    my_heads = pl.ds(mine_first, half_heads)
     my_rows = pl.ds(pl.multiple_of(d * rows, rows), rows)
 
     def around(place, offset, count):
@@ -85,7 +89,7 @@
     loads = [
         pltpu.make_async_copy(source, target, in_sem.at[place])
         for place, (source, target) in enumerate(
-            [(pair_in, pair), (wb_in, wb)]
+            [(wb_in, wb)]
             + [
                 (matrix, weights.at[h, place * width : (place + 1) * width, :])
                 for place, matrix in enumerate((wq, wk, wv, wg, wo))
@@ -93,7 +97,13 @@
             + [(mask_in, mask), (breaks_in, breaks)]
         )
     ]
-    loads[0].start()
+
+    def load_pair(group):
+        part = pl.ds(pl.multiple_of(group * block, block), block)
+        return pltpu.make_async_copy(pair_in.at[:, part], pair.at[:, part], pair_sem.at[group])
+
+    each(groups, lambda step: load_pair(far(step)).start(), start=1)
+    load_pair(d).start()
 
     barrier = pltpu.get_barrier_semaphore()
 
@@ -102,7 +112,7 @@
 
     each(groups, lambda step: greet(far(step), h), start=1)
     each(heads, lambda offset: greet(d, around(h, offset, heads)), start=1)
-    for load in loads[1:]:
+    for load in loads:
         load.start()
 
     taken = columns * rows
@@ -116,7 +126,7 @@
         part = nn(select, part.reshape(rows * block, channels)).astype(bf16)
         return part.reshape(columns, rows, channels)
 
-    loads[1].wait()
+    loads[0].wait()
     wb_all[h] = jnp.broadcast_to(wb[...].astype(f32), (rows, channels)).astype(bf16)
     pl.semaphore_wait(barrier, groups + heads - 2)
 
@@ -136,46 +146,61 @@
     all_x = all_copies(stage.at[pl.ds(0, groups - 1)], x_sem)
     all_w = all_copies(weights.at[pl.ds(0, heads - 1)], w_sem)
     all_wb = all_copies(wb_all.at[pl.ds(0, heads - 1)], wb_sem)
-    all_b = all_copies(bias.at[:, pl.ds(0, (groups - 1) * rows), :], b_sem)
+    all_b = all_copies(bias.at[pl.ds(0, half_heads), pl.ds(0, (groups - 1) * rows), :], b_sem)
+    pass_on = send(bias.at[my_heads], bias.at[my_heads], p_sem, d, partner)
     all_r = all_copies(landed.at[pl.ds(0, devices - 1)], r_sem)
 
     for offset in range(1, heads):
         send(wb_all.at[h], wb_all.at[h], wb_sem, d, around(h, offset, heads)).start()
 
-    loads[0].wait()
-
-    def scatter(step):
-        group = far(step)
-        stage[step] = selected(group)
-        send(stage.at[step], x.at[:, my_rows, :], x_sem, group, h).start()
-
-    each(groups, scatter, start=1)
+    def scatter(first, count):
+        steps = [first + index for index in range(count)]
+        for step in steps:
+            load_pair(far(step)).wait()
+        parts = [selected(far(step)) for step in steps]
+        for step, part in zip(steps, parts):
+            stage[step] = part
+        for step in steps:
+            send(stage.at[step], x.at[:, my_rows, :], x_sem, far(step), h).start()
+
+    half = groups // 2
+    if groups <= 8:
+        scatter(1, half)
+        scatter(1 + half, groups - 1 - half)
+    else:
+        pl.loop(1, groups)(lambda step: scatter(step, 1))
+    load_pair(d).wait()
     x[:, my_rows, :] = selected(d)
-    for load in loads[2:]:
+    for load in loads[1:]:
         load.wait()
     for offset in range(1, heads):
         send(weights.at[h], weights.at[h], w_sem, d, around(h, offset, heads)).start()
 
     average = jnp.full((channels, channels), 1.0 / channels, f32).astype(bf16)
-    bias_row = lax.rem(iota((heads * rows, LANES), 0), rows)
+    wb_shape = (half_heads * rows, rows * channels)
+    wb_place = lax.rem(iota(wb_shape, 0), rows) == iota(wb_shape, 1) // channels
+    chunk = min(rows, 4)
 
     def bias_block(place, arrived=True):
         span = lanes_at(place)
-        normed = [normalize(pair[row, span, :], average) for row in range(rows)]
+        normed = []
+        for row in range(0, rows, chunk):
+            piece = pair[row : row + chunk, span, :].reshape(chunk * LANES, channels)
+            piece = normalize(piece, average)
+            normed += [piece[line * LANES : (line + 1) * LANES] for line in range(chunk)]
         if not arrived:
             all_wb.wait_recv()
-        wb_rows = wb_all[...].reshape(heads * rows, channels)
-        found = jnp.zeros((heads * rows, LANES), f32)
-        for row in range(rows):
-            found = jnp.where(bias_row == row, nt(wb_rows, normed[row]), found)
-        bias[:, my_rows, span] = found.astype(bf16).reshape(heads, rows, LANES)
+        wb_rows = jnp.concatenate([wb_all[my_heads].reshape(half_heads * rows, channels)] * rows, axis=1)
+        wb_rows = jnp.where(wb_place, wb_rows, jnp.zeros((), bf16))
+        found = nt(wb_rows, jnp.concatenate(normed, axis=1))
+        bias[my_heads, my_rows, span] = found.astype(bf16).reshape(half_heads, rows, LANES)
 
     bias_block(0, arrived=False)
     if total > LANES:
         pl.loop(1, total // LANES)(bias_block)
 
     def share_bias(step):
-        part = bias.at[:, my_rows, :]
+        part = bias.at[my_heads, my_rows, :]
         send(part, part, b_sem, far(step), h).start()
 
     each(groups, share_bias, start=1)
@@ -201,10 +226,6 @@
     leave[...] = ones_where(
         first
         == lax.rem(entry, columns) * LANES + entry // columns * columns + second // LANES
-    )
-    arrive[...] = ones_where(
-        first
-        == entry // columns * rows + second // LANES * columns + lax.rem(entry, columns)
     )
 
     all_w.wait_recv()
@@ -235,40 +256,60 @@
             gate_t[first + column] = jax.nn.sigmoid(turned[wide_heads:, part]).astype(bf16)
 
     together = columns if total == LANES else 1
-    for first in range(0, columns, together):
-        project_in(first, together)
-
-    all_b.wait_recv()
+    for start in range(0, columns, together):
+        project_in(start, together)
+
     head_of_lane = iota((total, wide_heads), 1) // width
     head_of_row = iota((wide_heads, total), 0) // width
-
-    def attend(place):
-        span = lanes_at(place)
+    nothing = jnp.zeros((), bf16)
+
+    order = [around(mine_first, turn, heads) for turn in range(heads)]
+
+    def score(column, span):
+        upright = keys[column]
+        own = [jnp.where(head_of_lane == head, upright, nothing) for head in order]
+        return nt(jnp.concatenate(own, axis=0), query[column, span, :])
+
+    def share(scores, turn, span):
         penalty = jnp.where(chain_column[...] == chain_row[:1, span], 0.0, -chain_penalty)
-        added = [bias[head, :, span].astype(f32) + penalty for head in range(heads)]
-        present = keep[...] > 0.5
-
-        def attend_column(column):
-            upright, turned = keys[column], values_t[column]
-            nothing = jnp.zeros((), bf16)
-            own = [jnp.where(head_of_lane == head, upright, nothing) for head in range(heads)]
-            scores = nt(jnp.concatenate(own, axis=0), query[column, span, :])
-            shares = []
-            for head in range(heads):
-                mine = scores[head * total : (head + 1) * total] + added[head]
-                mine = jnp.where(present, mine, masked_score)
-                expo = jnp.exp(mine - jnp.max(mine, axis=0, keepdims=True))
-                scale = 1.0 / jnp.sum(expo, axis=0, keepdims=True)
-                shares.append((expo * scale).astype(bf16))
-            own = [jnp.where(head_of_row == head, turned, nothing) for head in range(heads)]
-            attended = nn(jnp.concatenate(own, axis=1), jnp.concatenate(shares, axis=0))
-            gated[column, :, span] = (
-                gate_t[column, :, span].astype(f32) * attended.astype(bf16).astype(f32)
-            ).astype(bf16)
-
-        each(columns, attend_column, most=columns if total == LANES else 1)
-
-    each(total // LANES, attend, most=1)
+        added = bias[order[turn], :, span].astype(f32) + penalty
+        mine = scores[turn * total : (turn + 1) * total] + added
+        mine = jnp.where(keep[...] > 0.5, mine, masked_score)
+        expo = jnp.exp(mine - jnp.max(mine, axis=0, keepdims=True))
+        scale = 1.0 / jnp.sum(expo, axis=0, keepdims=True)
+        return (expo * scale).astype(bf16)
+
+    def attend(column, shares, span):
+        turned = values_t[column]
+        own = [jnp.where(head_of_row == head, turned, nothing) for head in order]
+        attended = nn(jnp.concatenate(own, axis=1), jnp.concatenate(shares, axis=0))
+        gated[column, :, span] = (
+            gate_t[column, :, span].astype(f32) * attended.astype(bf16).astype(f32)
+        ).astype(bf16)
+
+    if total == LANES:
+        span = slice(0, LANES)
+        scores = [score(column, span) for column in range(columns)]
+        all_b.wait_recv()
+        pass_on.start()
+        shares = [[share(own, turn, span) for turn in range(half_heads)] for own in scores]
+        pass_on.wait_recv()
+        for column in range(columns):
+            later = [share(scores[column], turn, span) for turn in range(half_heads, heads)]
+            attend(column, shares[column] + later, span)
+    else:
+        all_b.wait_recv()
+        pass_on.start()
+        pass_on.wait_recv()
+
+        @pl.loop(0, total // LANES)
+        def _(place):
+            span = lanes_at(place)
+
+            @pl.loop(0, columns)
+            def _(column):
+                own = score(column, span)
+                attend(column, [share(own, turn, span) for turn in range(heads)], span)
 
     packed_lanes = columns * width
 
@@ -297,7 +338,11 @@
         each(groups, lambda step, head=head: give(far(step), head), start=1)
     each(heads, lambda offset: give(d, around(h, offset, heads)), start=1)
     landed[me] = result[me]
-    for copies in (all_x, all_w, all_wb, all_b):
+    arrive[...] = ones_where(
+        first
+        == entry // columns * rows + second // LANES * columns + lax.rem(entry, columns)
+    )
+    for copies in (all_x, all_w, all_wb, all_b, pass_on):
         copies.wait_send()
     all_r.wait_recv()
     sources = LANES // columns
@@ -351,7 +396,7 @@
             pltpu.VMEM((devices, rows, packed_lanes), bf16),
             pltpu.VMEM((columns * LANES, columns * LANES), bf16),
             pltpu.VMEM((columns * LANES, columns * LANES), bf16),
-            dma((9,)), dma((2,)), dma((2,)), dma((2,)), dma((2,)), dma((2,)),
+            dma((groups,)), dma((8,)), dma((2,)), dma((2,)), dma((2,)), dma((2,)), dma((2,)), dma((2,)),
         ],
         compiler_params=pltpu.CompilerParams(
             collective_id=0, has_side_effects=True, vmem_limit_bytes=52 * 2**20

time: 22 us -> 22.3 us (1.014)
    pallas_call x1, Pallas kernels: 21.2 us -> 21.4 us  [body(): pl.pallas_call(functools.partial(kernel, groups, heads), out_shape=pltpu....]
where the time goes in v3:
time: 22.3 us; the launch traced here: 22.1 us
  Pallas kernels  21.4 us (96%)
  local copies, waits for them, and re-layouts  0.66 us (3%)
    pallas_call x1, Pallas kernels, body(): pl.pallas_call(functools.partial(kernel, groups, heads), out_shape=pltpu....  21.4 us
    unnamed x1, local copies, waits for them, and re-layouts  0.66 us

profile of v3, /device:TPU:0, one launch (start us, length us, event | category | flops | bytes accessed | tf_op | source)
XLA Modules:
  0.0 22.1 jit_solution(14933282498876950231)
XLA Ops:
  0.0 21.4 %shard_map.91 = bf16[16,32,128]{2,1,0:T(8,128)(2,1)S(1)} custom-call(bf16[16,128,128]{2,1,0:T(8,128)(2,1)} %pair_in.1, s32[1,128]{1,0:T(1,128)} %bitcast.13, s32[1,128]{1,0:T(1,128)} %bitcast.14, bf16[32,128]{1,0:T(8,128)(2,1)} %bitcast.9, bf16[32,128]{1,0:T(8,128)(2,1)} %bitcast.10, bf16[32,128]{1,0:T(8,128)(2,1)} %bitcast.11, bf16[32,128]{1,0:T(8,128)(2,1)} %bitcast.12, ...), custom_call_target="tpu_custom_call" | custom-call | tf_op jit(solution)/shard_map/pallas_call | solution.py:371
  21.5 0.7 %copy.11 = bf16[16,128,32]{1,2,0:T(8,128)(2,1)} copy(bf16[16,128,32]{1,2,0:T(8,128)(2,1)S(1)} %bitcast.8) | data formatting | bytes 262144

commit v4 on v3

--- a/solution.py
+++ b/solution.py
@@ -77,6 +77,9 @@
     mine_first = lax.rem(h, 2) * half_heads
     partner = h + 1 - 2 * lax.rem(h, 2)
     my_heads = pl.ds(mine_first, half_heads)
+    halved = total == LANES
+    span_block = LANES // 2 if halved else LANES
+    half_groups = groups // 2
     my_rows = pl.ds(pl.multiple_of(d * rows, rows), rows)
 
     def around(place, offset, count):
@@ -219,13 +222,15 @@
     lane_source = lane // (columns * width) * width + lax.rem(lane, width)
     channel = iota((channels, out_lanes), 0)
 
-    ordered = columns * LANES
+    ordered = columns * span_block
     first = iota((ordered, ordered), 0)
     second = iota((1, ordered), 1)
-    entry = lax.rem(second, LANES)
+    entry = lax.rem(second, span_block)
     leave[...] = ones_where(
         first
-        == lax.rem(entry, columns) * LANES + entry // columns * columns + second // LANES
+        == lax.rem(entry, columns) * span_block
+        + entry // columns * columns
+        + second // span_block
     )
 
     all_w.wait_recv()
@@ -240,20 +245,30 @@
         for place in range(4)
     )
     wqk_t = jnp.concatenate([wq_t, wk_t], axis=0)
-    wvg_t = jnp.concatenate([wv_t, wg_t], axis=0)
     wide_heads = heads * width
 
     all_x.wait_recv()
     def project_in(first, count):
         normed = normalize(x[first : first + count].reshape(count * total, channels), average)
         upright = nt(normed, wqk_t)
-        turned = nt(wvg_t, normed)
+        turned = nt(wv_t, normed)
+        ordered_rows = normed
+        if halved:
+            ordered_rows = jnp.concatenate(
+                [
+                    normed[column * total + part * span_block :][:span_block]
+                    for part in range(2)
+                    for column in range(count)
+                ],
+                axis=0,
+            )
+        gates = jax.nn.sigmoid(nt(wg_t, ordered_rows)).astype(bf16)
         for column in range(count):
             part = slice(column * total, (column + 1) * total)
             query[first + column] = (upright[part, :wide_heads] * width ** (-0.5)).astype(bf16)
             keys[first + column] = upright[part, wide_heads:].astype(bf16)
-            values_t[first + column] = turned[:wide_heads, part].astype(bf16)
-            gate_t[first + column] = jax.nn.sigmoid(turned[wide_heads:, part]).astype(bf16)
+            values_t[first + column] = turned[:, part].astype(bf16)
+            gate_t[first + column] = gates[:, part]
 
     together = columns if total == LANES else 1
     for start in range(0, columns, together):
@@ -265,38 +280,108 @@
 
     order = [around(mine_first, turn, heads) for turn in range(heads)]
 
-    def score(column, span):
+    def key_rows(column):
         upright = keys[column]
         own = [jnp.where(head_of_lane == head, upright, nothing) for head in order]
-        return nt(jnp.concatenate(own, axis=0), query[column, span, :])
-
-    def share(scores, turn, span):
-        penalty = jnp.where(chain_column[...] == chain_row[:1, span], 0.0, -chain_penalty)
-        added = bias[order[turn], :, span].astype(f32) + penalty
-        mine = scores[turn * total : (turn + 1) * total] + added
-        mine = jnp.where(keep[...] > 0.5, mine, masked_score)
+        return jnp.concatenate(own, axis=0)
+
+    def value_rows(column):
+        turned = values_t[column]
+        own = [jnp.where(head_of_row == head, turned, nothing) for head in order]
+        return jnp.concatenate(own, axis=1)
+
+    def share(scores, turn, added, bound):
+        mine = jnp.minimum(scores[turn * total : (turn + 1) * total] + added, bound)
         expo = jnp.exp(mine - jnp.max(mine, axis=0, keepdims=True))
         scale = 1.0 / jnp.sum(expo, axis=0, keepdims=True)
         return (expo * scale).astype(bf16)
 
-    def attend(column, shares, span):
-        turned = values_t[column]
-        own = [jnp.where(head_of_row == head, turned, nothing) for head in order]
-        attended = nn(jnp.concatenate(own, axis=1), jnp.concatenate(shares, axis=0))
-        gated[column, :, span] = (
-            gate_t[column, :, span].astype(f32) * attended.astype(bf16).astype(f32)
-        ).astype(bf16)
-
-    if total == LANES:
-        span = slice(0, LANES)
-        scores = [score(column, span) for column in range(columns)]
+    def penalty(span):
+        return jnp.where(chain_column[...] == chain_row[:1, span], 0.0, -chain_penalty)
+
+    def gate_with(gate, attended):
+        return (gate.astype(f32) * attended.astype(bf16).astype(f32)).astype(bf16)
+
+    bound = jnp.where(keep[...] > 0.5, 3e38, masked_score)
+    packed_lanes = columns * width
+
+    def project(mine, first_group):
+        mine = nt(leave[...], mine).astype(bf16)
+        mine = jnp.concatenate(
+            [mine[part * span_block : (part + 1) * span_block] for part in range(columns)], axis=1
+        )
+        update = nn(mine, wide[...]).astype(bf16)
+        for part in range(span_block // rows):
+            for head in range(heads):
+                result[(first_group + part) * heads + head] = update[
+                    part * rows : (part + 1) * rows,
+                    head * packed_lanes : (head + 1) * packed_lanes,
+                ]
+
+    def give(pd, ph):
+        send(result.at[pd * heads + ph], landed.at[me], r_sem, pd, ph).start()
+
+    if halved:
+        near = d // half_groups
+        pairs = range(columns // 2)
+        key_pairs = [
+            jnp.concatenate([key_rows(2 * pair_of), key_rows(2 * pair_of + 1)], axis=1)
+            for pair_of in pairs
+        ]
+        value_pairs = [
+            jnp.concatenate([value_rows(2 * pair_of), value_rows(2 * pair_of + 1)], axis=0)
+            for pair_of in pairs
+        ]
+        left = iota((total, LANES), 1) < span_block
+        blank = jnp.zeros((span_block, wide_heads), bf16)
+
+        def score_pair(part, pair_of):
+            place = pl.ds(pl.multiple_of(part * span_block, span_block), span_block)
+            one = jnp.concatenate([query[2 * pair_of, place, :], blank], axis=1)
+            two = jnp.concatenate([blank, query[2 * pair_of + 1, place, :]], axis=1)
+            return nt(key_pairs[pair_of], jnp.concatenate([one, two], axis=0))
+
+        parts = (1 - near, near)
+        scores = [[score_pair(part, pair_of) for pair_of in pairs] for part in parts]
+        chains = penalty(slice(0, LANES))
+        kept = [iota((total, LANES), 1) // span_block == part for part in parts]
+
+        def added(turn):
+            whole = bias[order[turn]].astype(f32) + chains
+            turned = pltpu.roll(whole, span_block, 1)
+            return [jnp.where(own, whole, turned) for own in kept]
+
+        def shares_of(which, turn, extra):
+            return [share(scores[which][p], turn, extra[which], bound) for p in pairs]
+
+        def finish(which, shares):
+            part = parts[which]
+            mine = []
+            for p in pairs:
+                stacked = jnp.concatenate([shares[turn][p] for turn in range(heads)], axis=0)
+                both = nn(value_pairs[p], stacked)
+                attended = jnp.where(left, both[:wide_heads], both[wide_heads:])
+                mine.append(gate_with(gate_t[part * (columns // 2) + p], attended))
+            project(jnp.concatenate(mine, axis=1), part * half_groups)
+
         all_b.wait_recv()
         pass_on.start()
-        shares = [[share(own, turn, span) for turn in range(half_heads)] for own in scores]
+        extras = [added(turn) for turn in range(half_heads)]
+        shares = [shares_of(0, turn, extras[turn]) for turn in range(half_heads)]
         pass_on.wait_recv()
-        for column in range(columns):
-            later = [share(scores[column], turn, span) for turn in range(half_heads, heads)]
-            attend(column, shares[column] + later, span)
+        extras += [added(turn) for turn in range(half_heads, heads)]
+        shares += [shares_of(0, turn, extras[turn]) for turn in range(half_heads, heads)]
+        finish(0, shares)
+        in_half = d - near * half_groups
+        for head_offset in range(heads):
+            for step in range(half_groups):
+                group = parts[0] * half_groups + around(in_half, step, half_groups)
+                give(group, around(h, head_offset, heads))
+        finish(1, [shares_of(1, turn, extras[turn]) for turn in range(heads)])
+        for head_offset in range(heads):
+            for step in range(1, half_groups):
+                group = near * half_groups + around(in_half, step, half_groups)
+                give(group, around(h, head_offset, heads))
     else:
         all_b.wait_recv()
         pass_on.start()
@@ -308,36 +393,29 @@
 
             @pl.loop(0, columns)
             def _(column):
-                own = score(column, span)
-                attend(column, [share(own, turn, span) for turn in range(heads)], span)
-
-    packed_lanes = columns * width
-
-    def project(place):
-        span = lanes_at(place)
-        mine = jnp.concatenate([gated[column, :, span] for column in range(columns)], axis=1)
-        mine = nt(leave[...], mine).astype(bf16)
-        mine = jnp.concatenate(
-            [mine[part * LANES : (part + 1) * LANES] for part in range(columns)], axis=1
-        )
-        update = nn(mine, wide[...]).astype(bf16)
-        for part in range(LANES // rows):
-            for head in range(heads):
-                result[(place * (LANES // rows) + part) * heads + head] = update[
-                    part * rows : (part + 1) * rows,
-                    head * packed_lanes : (head + 1) * packed_lanes,
-                ]
-
-    each(total // LANES, project, most=1)
-
-    def give(pd, ph):
-        send(result.at[pd * heads + ph], landed.at[me], r_sem, pd, ph).start()
-
-    for head_offset in range(heads):
-        head = around(h, head_offset, heads)
-        each(groups, lambda step, head=head: give(far(step), head), start=1)
+                scores = nt(key_rows(column), query[column, span, :])
+                stacked = []
+                for turn in range(heads):
+                    added = bias[order[turn], :, span].astype(f32) + penalty(span)
+                    stacked.append(share(scores, turn, added, bound))
+                attended = nn(value_rows(column), jnp.concatenate(stacked, axis=0))
+                gated[column, :, span] = gate_with(gate_t[column, :, span], attended)
+
+        @pl.loop(0, total // LANES)
+        def _(place):
+            span = lanes_at(place)
+            mine = [gated[column, :, span] for column in range(columns)]
+            project(jnp.concatenate(mine, axis=1), place * (LANES // rows))
+
+        for head_offset in range(heads):
+            head = around(h, head_offset, heads)
+            each(groups, lambda step, head=head: give(far(step), head), start=1)
     each(heads, lambda offset: give(d, around(h, offset, heads)), start=1)
     landed[me] = result[me]
+    ordered = columns * LANES
+    first = iota((ordered, ordered), 0)
+    second = iota((1, ordered), 1)
+    entry = lax.rem(second, LANES)
     arrive[...] = ones_where(
         first
         == entry // columns * rows + second // LANES * columns + lax.rem(entry, columns)
@@ -366,6 +444,7 @@
     devices = groups * heads
     columns = total // devices
     packed_lanes = columns * width
+    span_block = LANES // 2 if total == LANES else LANES
     assert packed_lanes == LANES and columns * columns == rows
     dma = pltpu.SemaphoreType.DMA
     update = pl.pallas_call(
@@ -394,7 +473,7 @@
             pltpu.VMEM((columns, channels, total), bf16),
             pltpu.VMEM((devices, rows, packed_lanes), bf16),
             pltpu.VMEM((devices, rows, packed_lanes), bf16),
-            pltpu.VMEM((columns * LANES, columns * LANES), bf16),
+            pltpu.VMEM((columns * span_block, columns * span_block), bf16),
             pltpu.VMEM((columns * LANES, columns * LANES), bf16),
             dma((groups,)), dma((8,)), dma((2,)), dma((2,)), dma((2,)), dma((2,)), dma((2,)), dma((2,)),
         ],

time: 22.3 us -> 21.7 us (0.973)
  Pallas kernels: 21.4 us -> 20.9 us
    pallas_call x1, Pallas kernels: 21.4 us -> 20.9 us  [body(): pl.pallas_call(functools.partial(kernel, groups, heads), out_shape=pltpu....]
where the time goes in v4:
time: 21.7 us; the launch traced here: 21.6 us
  Pallas kernels  20.9 us (96%)
  local copies, waits for them, and re-layouts  0.66 us (3%)
    pallas_call x1, Pallas kernels, body(): pl.pallas_call(functools.partial(kernel, groups, heads), out_shape=pltpu....  20.9 us
    unnamed x1, local copies, waits for them, and re-layouts  0.66 us

profile of v4, /device:TPU:0, one launch (start us, length us, event | category | flops | bytes accessed | tf_op | source)
XLA Modules:
  0.0 21.6 jit_solution(10943556809522849681)
XLA Ops:
  0.0 20.9 %shard_map.91 = bf16[16,32,128]{2,1,0:T(8,128)(2,1)S(1)} custom-call(bf16[16,128,128]{2,1,0:T(8,128)(2,1)} %pair_in.1, s32[1,128]{1,0:T(1,128)} %bitcast.13, s32[1,128]{1,0:T(1,128)} %bitcast.14, bf16[32,128]{1,0:T(8,128)(2,1)} %bitcast.9, bf16[32,128]{1,0:T(8,128)(2,1)} %bitcast.10, bf16[32,128]{1,0:T(8,128)(2,1)} %bitcast.11, bf16[32,128]{1,0:T(8,128)(2,1)} %bitcast.12, ...), custom_call_target="tpu_custom_call" | custom-call | tf_op jit(solution)/shard_map/pallas_call | solution.py:450
  20.9 0.7 %copy.11 = bf16[16,128,32]{1,2,0:T(8,128)(2,1)} copy(bf16[16,128,32]{1,2,0:T(8,128)(2,1)S(1)} %bitcast.8) | data formatting | bytes 262144

commit v5 on v4

--- a/solution.py
+++ b/solution.py
@@ -63,7 +63,7 @@
     out,
     pair, mask, breaks, wb, stage, x, weights, wb_all, bias, wide, chain_column, chain_row, keep,
     query, keys, values_t, gate_t, gated, result, landed, leave, arrive,
-    pair_sem, in_sem, x_sem, w_sem, wb_sem, b_sem, p_sem, r_sem,
+    pair_sem, in_sem, x_sem, w_sem, wb_sem, b_sem, p_sem, f_sem, r_sem,
 ):
     rows, total, channels = pair.shape
     width = wq.shape[0]
@@ -151,7 +151,9 @@
     all_wb = all_copies(wb_all.at[pl.ds(0, heads - 1)], wb_sem)
     all_b = all_copies(bias.at[pl.ds(0, half_heads), pl.ds(0, (groups - 1) * rows), :], b_sem)
     pass_on = send(bias.at[my_heads], bias.at[my_heads], p_sem, d, partner)
-    all_r = all_copies(landed.at[pl.ds(0, devices - 1)], r_sem)
+    half_devices = devices // 2
+    first_r = all_copies(landed.at[pl.ds(0, half_devices)], f_sem)
+    all_r = all_copies(landed.at[pl.ds(0, (half_devices if halved else devices) - 1)], r_sem)
 
     for offset in range(1, heads):
         send(wb_all.at[h], wb_all.at[h], wb_sem, d, around(h, offset, heads)).start()
@@ -318,8 +320,8 @@
                     head * packed_lanes : (head + 1) * packed_lanes,
                 ]
 
-    def give(pd, ph):
-        send(result.at[pd * heads + ph], landed.at[me], r_sem, pd, ph).start()
+    def give(pd, ph, sems=r_sem):
+        send(result.at[pd * heads + ph], landed.at[me], sems, pd, ph).start()
 
     if halved:
         near = d // half_groups
@@ -376,7 +378,7 @@
         for head_offset in range(heads):
             for step in range(half_groups):
                 group = parts[0] * half_groups + around(in_half, step, half_groups)
-                give(group, around(h, head_offset, heads))
+                give(group, around(h, head_offset, heads), f_sem)
         finish(1, [shares_of(1, turn, extras[turn]) for turn in range(heads)])
         for head_offset in range(heads):
             for step in range(1, half_groups):
@@ -422,19 +424,32 @@
     )
     for copies in (all_x, all_w, all_wb, all_b, pass_on):
         copies.wait_send()
-    all_r.wait_recv()
-    sources = LANES // columns
-
-    def settle(place):
-        came = landed[pl.ds(place * sources, sources)].reshape(sources * rows, packed_lanes)
-        moved = tn(came, arrive[...]).astype(bf16)
+
+    def arranged(first_source, sources):
+        came = landed[pl.ds(first_source, sources)].reshape(sources * rows, packed_lanes)
+        if not halved:
+            return tn(came, arrive[...])
+        into = pl.multiple_of(first_source * rows, sources * rows)
+        return tn(came, arrive[pl.ds(into, sources * rows), :])
+
+    def settle(place, moved):
+        moved = moved.astype(bf16)
         for row in range(rows):
             part, line = row // columns, row % columns
             out[row, :, lanes_at(place)] = moved[
                 line * width : (line + 1) * width, part * LANES : (part + 1) * LANES
             ]
 
-    each(total // LANES, settle, most=1)
+    if halved:
+        first_r.wait_recv()
+        moved = arranged((1 - near) * half_devices, half_devices)
+        all_r.wait_recv()
+        settle(0, moved + arranged(near * half_devices, half_devices))
+        first_r.wait_send()
+    else:
+        all_r.wait_recv()
+        sources = LANES // columns
+        pl.loop(0, total // LANES)(lambda place: settle(place, arranged(place * sources, sources)))
     all_r.wait_send()
 
 
@@ -475,7 +490,7 @@
             pltpu.VMEM((devices, rows, packed_lanes), bf16),
             pltpu.VMEM((columns * span_block, columns * span_block), bf16),
             pltpu.VMEM((columns * LANES, columns * LANES), bf16),
-            dma((groups,)), dma((8,)), dma((2,)), dma((2,)), dma((2,)), dma((2,)), dma((2,)), dma((2,)),
+            dma((groups,)), dma((8,)), dma((2,)), dma((2,)), dma((2,)), dma((2,)), dma((2,)), dma((2,)), dma((2,)),
         ],
         compiler_params=pltpu.CompilerParams(
             collective_id=0, has_side_effects=True, vmem_limit_bytes=52 * 2**20

time: 21.7 us -> 21.8 us (level)
  no operation moved by 1% of the time
where the time goes in v5:
time: 21.8 us; the launch traced here: 21.6 us
  Pallas kernels  21 us (96%)
  local copies, waits for them, and re-layouts  0.66 us (3%)
    pallas_call x1, Pallas kernels, body(): pl.pallas_call(functools.partial(kernel, groups, heads), out_shape=pltpu....  21 us
    unnamed x1, local copies, waits for them, and re-layouts  0.66 us

profile of v5, /device:TPU:0, one launch (start us, length us, event | category | flops | bytes accessed | tf_op | source)
XLA Modules:
  0.0 21.6 jit_solution(1724811219236553007)
XLA Ops:
  0.0 21.0 %shard_map.91 = bf16[16,32,128]{2,1,0:T(8,128)(2,1)S(1)} custom-call(bf16[16,128,128]{2,1,0:T(8,128)(2,1)} %pair_in.1, s32[1,128]{1,0:T(1,128)} %bitcast.13, s32[1,128]{1,0:T(1,128)} %bitcast.14, bf16[32,128]{1,0:T(8,128)(2,1)} %bitcast.9, bf16[32,128]{1,0:T(8,128)(2,1)} %bitcast.10, bf16[32,128]{1,0:T(8,128)(2,1)} %bitcast.11, bf16[32,128]{1,0:T(8,128)(2,1)} %bitcast.12, ...), custom_call_target="tpu_custom_call" | custom-call | tf_op jit(solution)/shard_map/pallas_call | solution.py:465
  21.0 0.7 %copy.11 = bf16[16,128,32]{1,2,0:T(8,128)(2,1)} copy(bf16[16,128,32]{1,2,0:T(8,128)(2,1)S(1)} %bitcast.8) | data formatting | bytes 262144
